TPU v7x, 128 devices: a whole 4x4x4 slice. The times are simulated.
128 devices in a mesh: inst: 8 (over z, x_lo), blk: 16 (over y, x_hi, core).
Axes of the slice: x: 4 (x_hi: 2, x_lo: 2; x = x_hi * 2 + x_lo), y: 4, z: 4, core: 2. Of those that a mesh axis runs over, the one named last changes fastest.
Arguments:
- psi_start: float32 [8, 6, 128, 8192], P('inst', None, 'blk'), may hold values from -6 to 6
- coupling: float32 [8, 6, 6], P('inst'), may hold values from -2.5 to 2.5
- center: float32 [8, 128, 8192], P('inst', 'blk'), may hold values from 4 to 8
- spread: float32 [8, 128, 8192], P('inst', 'blk'), may hold values from 0.2 to 1
- source: float32 [8, 6, 128, 8192], P('inst', None, 'blk'), may hold values from -6 to 6
- wall_geo: float32 [8, 18, 32768], P('inst', None, 'blk'), may hold values from -6 to 6
- wall_cell: int32 [32768], P('blk'), may hold values from 0 to 65535
- wall_dest: int32 [32768, 1], P('blk'), may hold values from 0 to 15; in each aligned block of 2048 rows (0 to 2047, 2048 to 4095, ...) at most 256 rows name the same one
- wall_node: int32 [32768], P('blk'), may hold values from 0 to 4095
Outputs:
- psi_out: float32 [8, 6, 128, 8192], P('inst', None, 'blk')
- sensitivity: float32 [3, 65536], P(None, 'blk')
Inputs may be any that keep to these rules, and one draw needn't show every extreme that they name: `wall_dest`: among the 2048 wall faces of one grid block at most 256 go to one owner.
All inputs are finite; a program needn't handle non-finite values.
Results may differ from a plain program's by a relative error of at most 0.0001.
Values sent between devices are 32-bit elements; how exact they have to be, the bound alone decides.
No kernel may reach another device: no remote copies, remote signals or barrier semaphores. Data moves between devices by JAX's collectives and lax.ppermute only.
A program may use at most 192 MiB of HBM per device.

v0:
```python
import jax
import jax.numpy as jnp
from jax import lax
from jax.sharding import PartitionSpec as P

CAP = 256
NODE_DEV = 4096
ITERS = 2


def extended(shard, sides, width):
    for axis, dim in sides:
        devices, length = (lax.axis_size(axis), shard.shape[dim])
        up = [(i, (i + 1) % devices) for i in range(devices)]
        down = [(j, i) for i, j in up]
        last = lax.slice_in_dim(shard, length - width, length, axis=dim)
        leading = lax.slice_in_dim(shard, 0, width, axis=dim)
        before = lax.ppermute(last, axis, up)
        after = lax.ppermute(leading, axis, down)
        shard = jnp.concatenate([before, shard, after], axis=dim)
    return shard


def spectral_matrix(count):
    index = jnp.arange(count, dtype=jnp.int32)
    offset = index[:, None] - index[None, :]
    parity = (offset % 2).astype(jnp.float32)
    same = offset == 0
    angle = jnp.pi * offset.astype(jnp.float32) / count
    safe_angle = jnp.where(same, 1.0, angle)
    values = 0.5 * (1.0 - 2.0 * parity) / jnp.sin(safe_angle)
    return jnp.where(same, 0.0, values)


def spectral_source(psi, spec_mat):
    own_count = psi.shape[0]
    own_start = lax.axis_index("inst") * own_count
    piece = lax.all_gather(psi, "inst", axis=0, tiled=True)
    part_mat = lax.dynamic_slice(spec_mat, (0, own_start), (piece.shape[0], own_count))
    total = jnp.einsum("ji,jfxy->ifxy", part_mat, piece, precision=lax.Precision.HIGHEST)
    return 0.5 * total


def sweep(psi, coupling, center, spread, source, spec_mat):
    mixed = jnp.einsum("igf,igxy->ifxy", coupling, psi, precision=lax.Precision.HIGHEST)
    weighted = spread[:, None] * mixed
    rimmed = extended(weighted, (("blk", 2),), 1)
    beside = rimmed[:, :, 2:, :] + rimmed[:, :, :-2, :]
    padded = jnp.pad(weighted, ((0, 0), (0, 0), (0, 0), (1, 1)))
    beside = beside + padded[..., 2:] + padded[..., :-2]
    spectral = spectral_source(psi, spec_mat)
    update = center[:, None] * psi - beside + spectral - source
    return psi - (0.6 / center)[:, None] * update


def wall_partials(psi, wall_geo, wall_cell):
    inst_count, fields = (psi.shape[0], psi.shape[1])
    flat = psi.reshape(inst_count, fields, -1)
    picked = flat[:, :, wall_cell]
    geometry = wall_geo.reshape(inst_count, 3, fields, -1)
    partial_value = jnp.einsum("ikfe,ife->ike", geometry, picked, precision=lax.Precision.HIGHEST)
    return partial_value.reshape(inst_count * 3, -1)


def owner_slots(wall_dest, owners):
    dest = wall_dest[:, 0]
    onehot = (dest[:, None] == jnp.arange(owners, dtype=jnp.int32)[None, :]).astype(jnp.int32)
    before = jnp.cumsum(onehot, axis=0) - onehot
    rank = jnp.sum(before * onehot, axis=1)
    return (dest, rank)


def pack_slots(partial_value, dest, rank, wall_node, owners):
    rows = partial_value.shape[0]
    value_buf = jnp.zeros((rows, owners, CAP), jnp.float32).at[:, dest, rank].set(partial_value)
    node_buf = jnp.zeros((1, owners, CAP), jnp.int32).at[0, dest, rank].set(wall_node)
    return (value_buf, node_buf)


def unpack_slots(got_values, got_nodes):
    rows = got_values.shape[0]
    summed = jax.ops.segment_sum(
        got_values.reshape(rows, -1).T, got_nodes.reshape(-1), num_segments=NODE_DEV
    )
    return jnp.sum(summed.T.reshape(rows // 3, 3, NODE_DEV), axis=0)


def local(psi_start, coupling, center, spread, source, wall_geo, wall_cell, wall_dest, wall_node):
    owners = lax.axis_size("blk")
    spec_mat = spectral_matrix(psi_start.shape[0] * lax.axis_size("inst"))
    dest, rank = owner_slots(wall_dest, owners)
    sens_local = jnp.zeros((3, NODE_DEV), jnp.float32)
    psi = psi_start
    for step in range(ITERS):
        psi = sweep(psi, coupling, center, spread, source, spec_mat)
        partial_value = wall_partials(psi, wall_geo, wall_cell)
        value_buf, node_buf = pack_slots(partial_value, dest, rank, wall_node, owners)
        got_values, got_nodes = (
            lax.all_to_all(value_buf, "blk", split_axis=1, concat_axis=1, tiled=True),
            lax.all_to_all(node_buf, "blk", split_axis=1, concat_axis=1, tiled=True),
        )
        sens_local = sens_local + unpack_slots(got_values, got_nodes)
    sensitivity = lax.psum(sens_local, "inst")
    return (psi, sensitivity)


def solution(mesh):
    placed = (
        P("inst", None, "blk", None),
        P("inst", None, None),
        P("inst", "blk", None),
        P("inst", "blk", None),
        P("inst", None, "blk", None),
        P("inst", None, "blk"),
        P("blk"),
        P("blk", None),
        P("blk"),
    )
    return jax.shard_map(
        local,
        mesh=mesh,
        in_specs=placed,
        out_specs=(P("inst", None, "blk", None), P(None, "blk")),
        check_vma=False,
    )
```

profile of v0, /device:TPU:12, one launch (start us, length us, event | category | flops | bytes accessed | tf_op | source)
XLA Modules:
  0.0 807.7 jit_solution(17933240960903875595)
XLA Ops:
  8.6 4.3 fusion.4
  15.1 244.9 %all-gather.3.cloned.1.call-done = f32[8,6,8,8192]{3,2,1,0:T(8,128)} async-done(((f32[1,6,8,8192]{3,2,1,0:T(8,128)}), f32[8,6,8,8192]{3,2,1,0:T(8,128)}) %all-gather.3.cloned.1.call-update) | async-done | bytes 12582928 | tf_op jit(solution)/shard_map/all_gather | solution.py:38
  260.0 22.3 %fusion.2 = f32[1,6,8,8192]{3,0,2,1:T(1,128)S(1)} fusion(f32[8,6,8,8192]{3,2,1,0:T(8,128)} %all-gather.3.cloned.1.call-done, f32[8,8]{0,1:T(8,128)S(1)} %fusion.42, s32[]{:T(128)S(6)} %select_n.45), kind=kOutput, calls=%fused_computation.9 | convolution fusion | flops 37748736 | bytes 14156292 | tf_op jit(solution)/shard_map/ji,jfxy->ifxy/dot_general | solution.py:40
  282.4 5.1 copy_subtract_fusion
  289.6 4.5 reduce-window.6
  295.2 8.8 %scatter_custom_fusion.2 = s32[4096]{0:T(1024)} fusion(s32[2048]{0:T(1024)S(1)} %broadcast_select_fusion.1, s32[2048]{0:T(1024)} %param.17, s32[]{:T(128)} %constant.18.clone.1), kind=kCustom, calls=%fused_computation.69 | custom fusion | bytes 16896
  304.0 8.2 %all-to-all-start = ((s32[1,16,256]{2,0,1:T(1,128)}), s32[1,16,256]{2,0,1:T(1,128)S(1)}, u32[]{:S(2)}, u32[]{:S(2)}) async-start(s32[1,16,256]{2,0,1:T(1,128)} %bitcast.24), calls=%async_computation | async-start | bytes 32768 | tf_op jit(solution)/shard_map/all_to_all | solution.py:100
  312.6 3.1 copy.70
  320.6 17.3 %copy.53 = f32[6,65536]{0,1:T(8,128)} copy(f32[6,65536]{1,0:T(8,128)S(1)} %bitcast.101) | data formatting | bytes 3145728 | tf_op jit(solution)/shard_map/reshape | solution.py:58
  337.9 18.2 %gather_fusion = f32[2048,6]{1,0:T(8,128)} fusion(f32[6,65536]{0,1:T(8,128)} %copy.53, s32[2048]{0:T(1024)S(1)} %fusion.33), kind=kCustom, calls=%fused_computation | custom fusion | bytes 106496 | tf_op jit(solution)/shard_map/gather | solution.py:59
  356.1 16.6 %fusion.55 = f32[2048,1,3]{2,1,0:T(1,128)} fusion(f32[6,2048,1]{0,2,1:T(1,128)} %bitcast.120, f32[3,6,2048]{1,0,2:T(4,128)} %copy.70), kind=kOutput, calls=%fused_computation.97 | convolution fusion | flops 442368 | bytes 221184 | tf_op jit(solution)/shard_map/ikfe,ife->ike/dot_general | solution.py:61
  372.7 7.4 scatter_custom_fusion.3
  382.9 161.9 %all-gather.5.cloned.1.call-done = f32[8,6,8,8192]{3,2,1,0:T(8,128)} async-done(((f32[1,6,8,8192]{3,2,1,0:T(8,128)}), f32[8,6,8,8192]{3,2,1,0:T(8,128)}) %all-gather.5.cloned.1.call-update) | async-done | bytes 12582928 | tf_op jit(solution)/shard_map/all_gather | solution.py:38
  544.8 22.5 %fusion = f32[1,6,8,8192]{3,0,2,1:T(1,128)S(1)} fusion(f32[8,6,8,8192]{3,2,1,0:T(8,128)} %all-gather.5.cloned.1.call-done, f32[8,8]{0,1:T(8,128)S(1)} %fusion.42, s32[]{:T(128)S(6)} %select_n.45), kind=kOutput, calls=%fused_computation.7 | convolution fusion | flops 37748736 | bytes 14156292 | tf_op jit(solution)/shard_map/ji,jfxy->ifxy/dot_general | solution.py:40
  567.3 5.0 fusion.8
  572.3 16.5 %copy.56 = f32[6,65536]{0,1:T(8,128)} copy(f32[6,65536]{1,0:T(8,128)} %bitcast.102) | data formatting | bytes 3145728 | tf_op jit(solution)/shard_map/reshape | solution.py:58
  588.8 16.0 %gather_fusion.1 = f32[2048,6]{1,0:T(8,128)S(1)} fusion(f32[6,65536]{0,1:T(8,128)} %copy.56, s32[2048]{0:T(1024)S(1)} %fusion.33), kind=kCustom, calls=%fused_computation.1 | custom fusion | bytes 106496 | tf_op jit(solution)/shard_map/gather | solution.py:59
  604.8 7.3 all-to-all-start.1
  612.1 16.3 %fusion.56 = f32[2048,1,3]{2,1,0:T(1,128)} fusion(f32[6,2048,1]{0,2,1:T(1,128)S(1)} %bitcast.119, f32[3,6,2048]{1,0,2:T(4,128)} %copy.70), kind=kOutput, calls=%fused_computation.98 | convolution fusion | flops 442368 | bytes 221184 | tf_op jit(solution)/shard_map/ikfe,ife->ike/dot_general | solution.py:61
  628.3 6.5 scatter_custom_fusion.4
  636.0 7.6 all-to-all-start.2
  645.6 28.8 %scatter_custom_fusion = f32[4096,3]{1,0:T(8,128)} fusion(s32[4096]{0:T(1024)S(1)} %bitcast.117, f32[4096,3]{1,0:T(8,128)} %copy.55, f32[]{:T(128)} %constant.17.clone.1), kind=kCustom, calls=%fused_computation.47 | custom fusion | flops 12288 | bytes 49664 | tf_op jit(solution)/shard_map/scatter-add | solution.py:82
  678.4 28.7 %scatter_custom_fusion.1 = f32[4096,3]{1,0:T(8,128)} fusion(s32[4096]{0:T(1024)S(1)} %bitcast.118, f32[4096,3]{1,0:T(8,128)} %copy.58, f32[]{:T(128)} %constant.17.clone.1), kind=kCustom, calls=%fused_computation.45 | custom fusion | flops 12288 | bytes 49664 | tf_op jit(solution)/shard_map/scatter-add | solution.py:82
  710.3 89.1 %psum.7 = f32[3,4096]{0,1:T(8,128)S(1)} all-reduce(f32[3,4096]{0,1:T(8,128)} %add_bitcast_fusion), channel_id=1, replica_groups=mesh['inst'=8,'blk'=16] {'inst'}, use_global_device_ids=true, to_apply=%region_8.9 | all-reduce | flops 12288 | bytes 98304 | tf_op jit(solution)/shard_map/psum | solution.py:103
  (84 shorter events, 26.4 us)
Async XLA Ops:
  7.2 252.8 %all-gather.3.cloned.1.call-start = ((), (), s32[]{:S(2)}) async-start(), calls=%async_computation.3 | async-start | bytes 14155776 | tf_op jit(solution)/shard_map/all_gather | solution.py:38
  7.9 536.9 %all-gather.5.cloned.1.call-start = ((), (), s32[]{:S(2)}) async-start(), calls=%async_computation.4 | async-start | bytes 14155776 | tf_op jit(solution)/shard_map/all_gather | solution.py:38
  8.6 6.5 copy-start.10
  14.2 268.1 %collective-permute-start = (f32[1,6,1,8192]{3,1,2,0:T(8,128)S(1)}, f32[1,6,1,8192]{3,1,2,0:T(8,128)S(1)}, u32[]{:S(2)}, u32[]{:S(2)}) collective-permute-start(f32[1,6,1,8192]{3,1,2,0:T(8,128)S(1)} %get-tuple-element.12), channel_id=1, source_target_pairs={{1,0},{2,1},{3,2},{4,3},{5,4},{6,5},{7,6},{8,7},{9,8},{10,9},{11,1... | collective-permute-start | bytes 589832 | tf_op jit(solution)/shard_map/ppermute | solution.py:19
  14.3 268.0 %collective-permute-start.1 = (f32[1,6,1,8192]{3,1,2,0:T(8,128)S(1)}, f32[1,6,1,8192]{3,1,2,0:T(8,128)S(1)}, u32[]{:S(2)}, u32[]{:S(2)}) collective-permute-start(f32[1,6,1,8192]{3,1,2,0:T(8,128)S(1)} %get-tuple-element.13), channel_id=1, source_target_pairs={{0,1},{1,2},{2,3},{3,4},{4,5},{5,6},{6,7},{7,8},{8,9},{9,10},{10,1... | collective-permute-start | bytes 589832 | tf_op jit(solution)/shard_map/ppermute | solution.py:18
  260.0 22.3 %copy-start.2 = (f32[1,6,8,8192]{3,2,1,0:T(8,128)S(1)}, f32[1,6,8,8192]{3,2,1,0:T(8,128)}, u32[]{:S(2)}) copy-start(f32[1,6,8,8192]{3,2,1,0:T(8,128)} %param.9) | copy-start | bytes 4718596
  260.0 22.4 %copy-start.4 = (f32[1,6,8,8192]{3,1,2,0:T(8,128)S(1)}, f32[1,6,8,8192]{3,1,2,0:T(8,128)}, u32[]{:S(2)}) copy-start(f32[1,6,8,8192]{3,1,2,0:T(8,128)} %copy-done.3) | copy-start | bytes 4718596
  260.0 22.4 %copy-start.8 = (f32[1,6,8,8192]{3,2,1,0:T(8,128)S(1)}, f32[1,6,8,8192]{3,2,1,0:T(8,128)}, u32[]{:S(2)}) copy-start(f32[1,6,8,8192]{3,2,1,0:T(8,128)} %param.13) | copy-start | bytes 4718596
  289.5 5.4 copy-start.16
  289.5 5.5 copy-start.19
  289.5 22.6 %copy-start.12 = (f32[1,18,2048]{2,0,1:T(1,128)S(1)}, f32[1,18,2048]{2,0,1:T(1,128)}, u32[]{:S(2)}) copy-start(f32[1,18,2048]{2,0,1:T(1,128)} %param.14) | copy-start | bytes 442372
  304.0 300.8 %all-to-all-start = ((s32[1,16,256]{2,0,1:T(1,128)}), s32[1,16,256]{2,0,1:T(1,128)S(1)}, u32[]{:S(2)}, u32[]{:S(2)}) async-start(s32[1,16,256]{2,0,1:T(1,128)} %bitcast.24), calls=%async_computation | async-start | bytes 32768 | tf_op jit(solution)/shard_map/all_to_all | solution.py:100
  312.5 3.3 copy-start.17
  312.6 3.4 copy-start.15
  312.6 3.4 copy-start.11
  312.6 3.4 copy-start.14
  320.1 247.2 %collective-permute-start.2 = (f32[1,6,1,8192]{3,1,2,0:T(8,128)}, f32[1,6,1,8192]{3,1,2,0:T(8,128)S(1)}, u32[]{:S(2)}, u32[]{:S(2)}) collective-permute-start(f32[1,6,1,8192]{3,1,2,0:T(8,128)} %get-tuple-element.10), channel_id=1, source_target_pairs={{1,0},{2,1},{3,2},{4,3},{5,4},{6,5},{7,6},{8,7},{9,8},{10,9},{11,1... | collective-permute-start | bytes 589832 | tf_op jit(solution)/shard_map/ppermute | solution.py:19
  320.4 246.8 %collective-permute-start.3 = (f32[1,6,1,8192]{3,1,2,0:T(8,128)S(1)}, f32[1,6,1,8192]{3,1,2,0:T(8,128)S(1)}, u32[]{:S(2)}, u32[]{:S(2)}) collective-permute-start(f32[1,6,1,8192]{3,1,2,0:T(8,128)S(1)} %get-tuple-element.11), channel_id=1, source_target_pairs={{0,1},{1,2},{2,3},{3,4},{4,5},{5,6},{6,7},{7,8},{8,9},{9,10},{10,1... | collective-permute-start | bytes 589832 | tf_op jit(solution)/shard_map/ppermute | solution.py:18
  544.8 22.5 %copy-start.6 = (f32[1,6,8,8192]{3,1,2,0:T(8,128)S(1)}, f32[1,6,8,8192]{3,1,2,0:T(8,128)}, u32[]{:S(2)}) copy-start(f32[1,6,8,8192]{3,1,2,0:T(8,128)} %copy-done.5) | copy-start | bytes 4718596
  544.8 22.5 %copy-start.9 = (f32[1,6,8,8192]{3,2,1,0:T(8,128)S(1)}, f32[1,6,8,8192]{3,2,1,0:T(8,128)}, u32[]{:S(2)}) copy-start(f32[1,6,8,8192]{3,2,1,0:T(8,128)} %param.13) | copy-start | bytes 4718596
  604.8 31.2 %all-to-all-start.1 = ((f32[3,16,256]{2,0,1:T(4,128)}), f32[3,16,256]{2,0,1:T(4,128)S(1)}, u32[]{:S(2)}, u32[]{:S(2)}) async-start(f32[3,16,256]{2,0,1:T(4,128)} %copy.54), calls=%async_computation.1 | async-start | bytes 131072 | tf_op jit(solution)/shard_map/all_to_all | solution.py:99
  636.0 40.4 %all-to-all-start.2 = ((f32[3,16,256]{2,0,1:T(4,128)}), f32[3,16,256]{2,0,1:T(4,128)S(1)}, u32[]{:S(2)}, u32[]{:S(2)}) async-start(f32[3,16,256]{2,0,1:T(4,128)} %copy.57), calls=%async_computation.2 | async-start | bytes 131072 | tf_op jit(solution)/shard_map/all_to_all | solution.py:99
  643.6 30.8 %copy-start = (f32[1,6,8,8192]{3,1,2,0:T(8,128)S(1)}, f32[1,6,8,8192]{3,1,2,0:T(8,128)}, u32[]{:S(2)}) copy-start(f32[1,6,8,8192]{3,1,2,0:T(8,128)} %fusion.8) | copy-start | bytes 4718596
  676.4 30.7 %copy-start.7 = (f32[4096,3]{1,0:T(8,128)S(1)}, f32[4096,3]{1,0:T(8,128)}, u32[]{:S(2)}) copy-start(f32[4096,3]{1,0:T(8,128)} %scatter_custom_fusion) | copy-start | bytes 147460
  (5 other events, 9.4 us)
Sparse Core Ops, SparseCore 0:
  9.7 250.3 all-gather.2
  289.7 255.0 all-gather.4
where the time goes:
time: 812 us; the launch traced here: 808 us
  waiting for transfers between devices  408 us (50%)
  local copies, waits for them, and re-layouts  112 us (14%)
  blocking collectives  89.1 us (11%)
  matrix products  83.9 us (10%)
  other arithmetic  76.5 us (9%)
  starting transfers between devices  24.3 us (3%)
  between operations  14.7 us (2%)
    all_gather x2, waiting for transfers between devices, spectral_source(): piece = lax.all_gather(psi, 'inst', axis=0, tiled=True)  407 us
    psum x1, blocking collectives, local(): sensitivity = lax.psum(sens_local, 'inst')  89.1 us
    scatter-add x2, other arithmetic, unpack_slots(): jax.ops.segment_sum(got_values.reshape(rows, -1).T, got_nodes.reshape(-1)...  57.5 us
    dot_general x2, matrix products, spectral_source(): jnp.einsum('ji,jfxy->ifxy', part_mat, piece, precision=lax.Precision.HIGH...  44.8 us
    gather x2, local copies, waits for them, and re-layouts, wall_partials(): picked = flat[:, :, wall_cell]  34.2 us
    reshape x2, local copies, waits for them, and re-layouts, wall_partials(): flat = psi.reshape(inst_count, fields, -1)  33.8 us
    dot_general x2, matrix products, wall_partials(): jnp.einsum('ikfe,ife->ike', geometry, picked, precision=lax.Precision.HIG...  32.8 us
    unnamed x45, local copies, waits for them, and re-layouts  29.3 us
  transfers between devices with their start and end apart: 9, of which 2 were waited for; matrix products, arithmetic and copies ran while one was open for 28% of the time, Pallas kernels for 0%

commit v1 on v0

--- a/solution.py
+++ b/solution.py
@@ -6,6 +6,11 @@
 CAP = 256
 NODE_DEV = 4096
 ITERS = 2
+
+
+def summed_here(x, axis):
+    parts = lax.all_gather(x, axis)
+    return jnp.sum(parts, axis=0)
 
 
 def extended(shard, sides, width):
@@ -100,7 +105,7 @@
             lax.all_to_all(node_buf, "blk", split_axis=1, concat_axis=1, tiled=True),
         )
         sens_local = sens_local + unpack_slots(got_values, got_nodes)
-    sensitivity = lax.psum(sens_local, "inst")
+    sensitivity = summed_here(sens_local, "inst")
     return (psi, sensitivity)
 
 

time: 812 us -> 755 us (0.930)
  blocking collectives: 89.1 us -> 30.2 us
    psum x1 -> x0, blocking collectives: 89.1 us -> none  [local(): sensitivity = lax.psum(sens_local, 'inst')]
    all_gather x0 -> x1, blocking collectives: none -> 30.2 us  [summed_here(): parts = lax.all_gather(x, axis)]
  transfers between devices with their start and end apart: 9 -> 9, of which waited for: 2 -> 2; matrix products, arithmetic and copies ran while one was open for 28% -> 30% of each run, Pallas kernels for 0% -> 0%
where the time goes in v1:
time: 755 us; the launch traced here: 750 us
  waiting for transfers between devices  408 us (54%)
  local copies, waits for them, and re-layouts  113 us (15%)
  matrix products  83.9 us (11%)
  other arithmetic  77.2 us (10%)
  blocking collectives  30.2 us (4%)
  starting transfers between devices  24.3 us (3%)
  between operations  14.7 us (2%)
    all_gather x2, waiting for transfers between devices, spectral_source(): piece = lax.all_gather(psi, 'inst', axis=0, tiled=True)  407 us
    scatter-add x2, other arithmetic, unpack_slots(): jax.ops.segment_sum(got_values.reshape(rows, -1).T, got_nodes.reshape(-1)...  57.5 us
    dot_general x2, matrix products, spectral_source(): jnp.einsum('ji,jfxy->ifxy', part_mat, piece, precision=lax.Precision.HIGH...  44.8 us
    gather x2, local copies, waits for them, and re-layouts, wall_partials(): picked = flat[:, :, wall_cell]  34.2 us
    reshape x2, local copies, waits for them, and re-layouts, wall_partials(): flat = psi.reshape(inst_count, fields, -1)  33.8 us
    dot_general x2, matrix products, wall_partials(): jnp.einsum('ikfe,ife->ike', geometry, picked, precision=lax.Precision.HIG...  32.8 us
    unnamed x45, local copies, waits for them, and re-layouts  30.2 us
    all_gather x1, blocking collectives, summed_here(): parts = lax.all_gather(x, axis)  30.2 us
  transfers between devices with their start and end apart: 9, of which 2 were waited for; matrix products, arithmetic and copies ran while one was open for 30% of the time, Pallas kernels for 0%

profile of v1, /device:TPU:12, one launch (start us, length us, event | category | flops | bytes accessed | tf_op | source)
XLA Modules:
  0.0 750.5 jit_solution(13407548063474160628)
XLA Ops:
  8.6 4.3 fusion.4
  15.1 244.9 %all-gather.5.cloned.1.call-done = f32[8,6,8,8192]{3,2,1,0:T(8,128)} async-done(((f32[1,6,8,8192]{3,2,1,0:T(8,128)}), f32[8,6,8,8192]{3,2,1,0:T(8,128)}) %all-gather.5.cloned.1.call-update) | async-done | bytes 12582928 | tf_op jit(solution)/shard_map/all_gather | solution.py:43
  260.0 22.3 %fusion.2 = f32[1,6,8,8192]{3,0,2,1:T(1,128)S(1)} fusion(f32[8,6,8,8192]{3,2,1,0:T(8,128)} %all-gather.5.cloned.1.call-done, f32[8,8]{0,1:T(8,128)S(1)} %fusion.42, s32[]{:T(128)S(6)} %select_n.45), kind=kOutput, calls=%fused_computation.9 | convolution fusion | flops 37748736 | bytes 14156292 | tf_op jit(solution)/shard_map/ji,jfxy->ifxy/dot_general | solution.py:45
  282.4 5.1 copy_subtract_fusion
  289.6 4.5 reduce-window.6
  295.2 8.8 %scatter_custom_fusion.2 = s32[4096]{0:T(1024)} fusion(s32[2048]{0:T(1024)S(1)} %broadcast_select_fusion.1, s32[2048]{0:T(1024)} %param.17, s32[]{:T(128)} %constant.18.clone.1), kind=kCustom, calls=%fused_computation.69 | custom fusion | bytes 16896
  304.0 8.2 %all-to-all-start = ((s32[1,16,256]{2,0,1:T(1,128)}), s32[1,16,256]{2,0,1:T(1,128)S(1)}, u32[]{:S(2)}, u32[]{:S(2)}) async-start(s32[1,16,256]{2,0,1:T(1,128)} %bitcast.24), calls=%async_computation | async-start | bytes 32768 | tf_op jit(solution)/shard_map/all_to_all | solution.py:105
  312.6 3.1 copy.72
  320.6 17.3 %copy.53 = f32[6,65536]{0,1:T(8,128)} copy(f32[6,65536]{1,0:T(8,128)S(1)} %bitcast.103) | data formatting | bytes 3145728 | tf_op jit(solution)/shard_map/reshape | solution.py:63
  337.9 18.2 %gather_fusion = f32[2048,6]{1,0:T(8,128)} fusion(f32[6,65536]{0,1:T(8,128)} %copy.53, s32[2048]{0:T(1024)S(1)} %fusion.33), kind=kCustom, calls=%fused_computation | custom fusion | bytes 106496 | tf_op jit(solution)/shard_map/gather | solution.py:64
  356.1 16.6 %fusion.55 = f32[2048,1,3]{2,1,0:T(1,128)} fusion(f32[6,2048,1]{0,2,1:T(1,128)} %bitcast.122, f32[3,6,2048]{1,0,2:T(4,128)} %copy.72), kind=kOutput, calls=%fused_computation.97 | convolution fusion | flops 442368 | bytes 221184 | tf_op jit(solution)/shard_map/ikfe,ife->ike/dot_general | solution.py:66
  372.7 7.4 scatter_custom_fusion.3
  382.9 161.9 %all-gather.7.cloned.1.call-done = f32[8,6,8,8192]{3,2,1,0:T(8,128)} async-done(((f32[1,6,8,8192]{3,2,1,0:T(8,128)}), f32[8,6,8,8192]{3,2,1,0:T(8,128)}) %all-gather.7.cloned.1.call-update) | async-done | bytes 12582928 | tf_op jit(solution)/shard_map/all_gather | solution.py:43
  544.8 22.5 %fusion = f32[1,6,8,8192]{3,0,2,1:T(1,128)S(1)} fusion(f32[8,6,8,8192]{3,2,1,0:T(8,128)} %all-gather.7.cloned.1.call-done, f32[8,8]{0,1:T(8,128)S(1)} %fusion.42, s32[]{:T(128)S(6)} %select_n.45), kind=kOutput, calls=%fused_computation.7 | convolution fusion | flops 37748736 | bytes 14156292 | tf_op jit(solution)/shard_map/ji,jfxy->ifxy/dot_general | solution.py:45
  567.3 5.0 fusion.8
  572.3 16.5 %copy.56 = f32[6,65536]{0,1:T(8,128)} copy(f32[6,65536]{1,0:T(8,128)} %bitcast.104) | data formatting | bytes 3145728 | tf_op jit(solution)/shard_map/reshape | solution.py:63
  588.8 16.0 %gather_fusion.1 = f32[2048,6]{1,0:T(8,128)S(1)} fusion(f32[6,65536]{0,1:T(8,128)} %copy.56, s32[2048]{0:T(1024)S(1)} %fusion.33), kind=kCustom, calls=%fused_computation.1 | custom fusion | bytes 106496 | tf_op jit(solution)/shard_map/gather | solution.py:64
  604.8 7.3 all-to-all-start.1
  612.1 16.3 %fusion.56 = f32[2048,1,3]{2,1,0:T(1,128)} fusion(f32[6,2048,1]{0,2,1:T(1,128)S(1)} %bitcast.121, f32[3,6,2048]{1,0,2:T(4,128)} %copy.72), kind=kOutput, calls=%fused_computation.98 | convolution fusion | flops 442368 | bytes 221184 | tf_op jit(solution)/shard_map/ikfe,ife->ike/dot_general | solution.py:66
  628.3 6.5 scatter_custom_fusion.4
  636.0 7.6 %all-to-all-start.2 = ((f32[3,16,256]{2,0,1:T(4,128)}), f32[3,16,256]{2,0,1:T(4,128)S(1)}, u32[]{:S(2)}, u32[]{:S(2)}) async-start(f32[3,16,256]{2,0,1:T(4,128)} %copy.57), calls=%async_computation.2 | async-start | bytes 131072 | tf_op jit(solution)/shard_map/all_to_all | solution.py:104
  645.6 28.8 %scatter_custom_fusion = f32[4096,3]{1,0:T(8,128)} fusion(s32[4096]{0:T(1024)S(1)} %bitcast.119, f32[4096,3]{1,0:T(8,128)} %copy.55, f32[]{:T(128)} %constant.17.clone.1), kind=kCustom, calls=%fused_computation.47 | custom fusion | flops 12288 | bytes 49664 | tf_op jit(solution)/shard_map/scatter-add | solution.py:87
  678.4 28.7 %scatter_custom_fusion.1 = f32[4096,3]{1,0:T(8,128)} fusion(s32[4096]{0:T(1024)S(1)} %bitcast.120, f32[4096,3]{1,0:T(8,128)} %copy.58, f32[]{:T(128)} %constant.17.clone.1), kind=kCustom, calls=%fused_computation.45 | custom fusion | flops 12288 | bytes 49664 | tf_op jit(solution)/shard_map/scatter-add | solution.py:87
  712.5 30.2 %all-gather.1 = f32[8,3,4096]{2,1,0:T(4,128)S(1)} all-gather(f32[1,3,4096]{2,1,0:T(4,128)S(1)} %copy.59), channel_id=2, replica_groups=mesh['inst'=8,'blk'=16] {'inst'}, dimensions={0}, use_global_device_ids=true | all-gather | bytes 442368 | tf_op jit(solution)/shard_map/all_gather | solution.py:12
  (85 shorter events, 28.0 us)
Async XLA Ops:
  7.2 252.8 %all-gather.5.cloned.1.call-start = ((), (), s32[]{:S(2)}) async-start(), calls=%async_computation.3 | async-start | bytes 14155776 | tf_op jit(solution)/shard_map/all_gather | solution.py:43
  7.9 536.9 %all-gather.7.cloned.1.call-start = ((), (), s32[]{:S(2)}) async-start(), calls=%async_computation.4 | async-start | bytes 14155776 | tf_op jit(solution)/shard_map/all_gather | solution.py:43
  8.6 6.5 copy-start.10
  14.2 268.1 %collective-permute-start = (f32[1,6,1,8192]{3,1,2,0:T(8,128)S(1)}, f32[1,6,1,8192]{3,1,2,0:T(8,128)S(1)}, u32[]{:S(2)}, u32[]{:S(2)}) collective-permute-start(f32[1,6,1,8192]{3,1,2,0:T(8,128)S(1)} %get-tuple-element.12), channel_id=1, source_target_pairs={{1,0},{2,1},{3,2},{4,3},{5,4},{6,5},{7,6},{8,7},{9,8},{10,9},{11,1... | collective-permute-start | bytes 589832 | tf_op jit(solution)/shard_map/ppermute | solution.py:24
  14.3 268.0 %collective-permute-start.1 = (f32[1,6,1,8192]{3,1,2,0:T(8,128)S(1)}, f32[1,6,1,8192]{3,1,2,0:T(8,128)S(1)}, u32[]{:S(2)}, u32[]{:S(2)}) collective-permute-start(f32[1,6,1,8192]{3,1,2,0:T(8,128)S(1)} %get-tuple-element.13), channel_id=1, source_target_pairs={{0,1},{1,2},{2,3},{3,4},{4,5},{5,6},{6,7},{7,8},{8,9},{9,10},{10,1... | collective-permute-start | bytes 589832 | tf_op jit(solution)/shard_map/ppermute | solution.py:23
  260.0 22.3 %copy-start.2 = (f32[1,6,8,8192]{3,2,1,0:T(8,128)S(1)}, f32[1,6,8,8192]{3,2,1,0:T(8,128)}, u32[]{:S(2)}) copy-start(f32[1,6,8,8192]{3,2,1,0:T(8,128)} %param.9) | copy-start | bytes 4718596
  260.0 22.4 %copy-start.4 = (f32[1,6,8,8192]{3,1,2,0:T(8,128)S(1)}, f32[1,6,8,8192]{3,1,2,0:T(8,128)}, u32[]{:S(2)}) copy-start(f32[1,6,8,8192]{3,1,2,0:T(8,128)} %copy-done.3) | copy-start | bytes 4718596
  260.0 22.4 %copy-start.8 = (f32[1,6,8,8192]{3,2,1,0:T(8,128)S(1)}, f32[1,6,8,8192]{3,2,1,0:T(8,128)}, u32[]{:S(2)}) copy-start(f32[1,6,8,8192]{3,2,1,0:T(8,128)} %param.13) | copy-start | bytes 4718596
  289.5 5.4 copy-start.16
  289.5 5.5 copy-start.19
  289.5 22.6 %copy-start.12 = (f32[1,18,2048]{2,0,1:T(1,128)S(1)}, f32[1,18,2048]{2,0,1:T(1,128)}, u32[]{:S(2)}) copy-start(f32[1,18,2048]{2,0,1:T(1,128)} %param.14) | copy-start | bytes 442372
  304.0 300.8 %all-to-all-start = ((s32[1,16,256]{2,0,1:T(1,128)}), s32[1,16,256]{2,0,1:T(1,128)S(1)}, u32[]{:S(2)}, u32[]{:S(2)}) async-start(s32[1,16,256]{2,0,1:T(1,128)} %bitcast.24), calls=%async_computation | async-start | bytes 32768 | tf_op jit(solution)/shard_map/all_to_all | solution.py:105
  312.5 3.3 copy-start.17
  312.6 3.4 copy-start.15
  312.6 3.4 copy-start.11
  312.6 3.4 copy-start.14
  320.1 247.2 %collective-permute-start.2 = (f32[1,6,1,8192]{3,1,2,0:T(8,128)}, f32[1,6,1,8192]{3,1,2,0:T(8,128)S(1)}, u32[]{:S(2)}, u32[]{:S(2)}) collective-permute-start(f32[1,6,1,8192]{3,1,2,0:T(8,128)} %get-tuple-element.10), channel_id=1, source_target_pairs={{1,0},{2,1},{3,2},{4,3},{5,4},{6,5},{7,6},{8,7},{9,8},{10,9},{11,1... | collective-permute-start | bytes 589832 | tf_op jit(solution)/shard_map/ppermute | solution.py:24
  320.4 246.8 %collective-permute-start.3 = (f32[1,6,1,8192]{3,1,2,0:T(8,128)S(1)}, f32[1,6,1,8192]{3,1,2,0:T(8,128)S(1)}, u32[]{:S(2)}, u32[]{:S(2)}) collective-permute-start(f32[1,6,1,8192]{3,1,2,0:T(8,128)S(1)} %get-tuple-element.11), channel_id=1, source_target_pairs={{0,1},{1,2},{2,3},{3,4},{4,5},{5,6},{6,7},{7,8},{8,9},{9,10},{10,1... | collective-permute-start | bytes 589832 | tf_op jit(solution)/shard_map/ppermute | solution.py:23
  544.8 22.5 %copy-start.6 = (f32[1,6,8,8192]{3,1,2,0:T(8,128)S(1)}, f32[1,6,8,8192]{3,1,2,0:T(8,128)}, u32[]{:S(2)}) copy-start(f32[1,6,8,8192]{3,1,2,0:T(8,128)} %copy-done.5) | copy-start | bytes 4718596
  544.8 22.5 %copy-start.9 = (f32[1,6,8,8192]{3,2,1,0:T(8,128)S(1)}, f32[1,6,8,8192]{3,2,1,0:T(8,128)}, u32[]{:S(2)}) copy-start(f32[1,6,8,8192]{3,2,1,0:T(8,128)} %param.13) | copy-start | bytes 4718596
  604.8 31.2 %all-to-all-start.1 = ((f32[3,16,256]{2,0,1:T(4,128)}), f32[3,16,256]{2,0,1:T(4,128)S(1)}, u32[]{:S(2)}, u32[]{:S(2)}) async-start(f32[3,16,256]{2,0,1:T(4,128)} %copy.54), calls=%async_computation.1 | async-start | bytes 131072 | tf_op jit(solution)/shard_map/all_to_all | solution.py:104
  636.0 40.4 %all-to-all-start.2 = ((f32[3,16,256]{2,0,1:T(4,128)}), f32[3,16,256]{2,0,1:T(4,128)S(1)}, u32[]{:S(2)}, u32[]{:S(2)}) async-start(f32[3,16,256]{2,0,1:T(4,128)} %copy.57), calls=%async_computation.2 | async-start | bytes 131072 | tf_op jit(solution)/shard_map/all_to_all | solution.py:104
  643.6 30.8 %copy-start = (f32[1,6,8,8192]{3,1,2,0:T(8,128)S(1)}, f32[1,6,8,8192]{3,1,2,0:T(8,128)}, u32[]{:S(2)}) copy-start(f32[1,6,8,8192]{3,1,2,0:T(8,128)} %fusion.8) | copy-start | bytes 4718596
  676.4 30.7 %copy-start.7 = (f32[4096,3]{1,0:T(8,128)S(1)}, f32[4096,3]{1,0:T(8,128)}, u32[]{:S(2)}) copy-start(f32[4096,3]{1,0:T(8,128)} %scatter_custom_fusion) | copy-start | bytes 147460
  (5 other events, 9.4 us)
Sparse Core Ops, SparseCore 0:
  9.7 250.3 all-gather.4
  289.7 255.0 all-gather.6
